TPU v7x, 32 devices: a whole 2x2x4 slice. The times are simulated.
32 devices in a mesh: section: 4 (over y, x), tensor: 8 (over z, core).
Axes of the slice: x: 2, y: 2, z: 4, core: 2. Of those that a mesh axis runs over, the one named last changes fastest.
Arguments:
- x_in: bfloat16 [4, 512, 4096], P('section', 'tensor'), may hold values from -40 to 40
- grad_out: bfloat16 [4, 512, 4096], P('section', 'tensor'), may hold values from -50 to 50
- gain: float32 [4, 4096], P('section'), may hold values from 0.5 to 1.5
- w_val: bfloat16 [4, 4096, 4096], P('section', 'tensor'), may hold values from -0.09375 to 0.09375
- w_out: bfloat16 [4, 4096, 4096], P('section', 'tensor'), may hold values from -0.09375 to 0.09375
- filt: float32 [4, 3, 4096], P('section', None, 'tensor'), may hold values from -3 to 3
- tail: bfloat16 [4, 2, 4096], P('section', None, 'tensor'), may hold values from -6 to 6
- micro_index: int32 [4], P('section'), may hold values from 0 to 15
Outputs:
- grad_in: bfloat16 [4, 512, 4096], P('section', 'tensor')
- grad_w_val: bfloat16 [4, 4096, 4096], P('section', 'tensor')
- grad_w_out: bfloat16 [4, 4096, 4096], P('section', 'tensor')
- grad_filter: float32 [4, 3, 4096], P('section', None, 'tensor')
- grad_tail: float32 [4, 2, 4096], P('section', None, 'tensor')
- grad_gain: float32 [4, 4096], P('section')
All inputs are finite; a program needn't handle non-finite values.
Results may differ from a plain program's by a relative error of at most 0.023.
Values may be sent and summed in bfloat16 or wider, within the bound.
A program may use at most 64 MiB of HBM per device.

v0:
```python
import jax
import jax.numpy as jnp
from jax import lax
from jax.sharding import PartitionSpec as P

TAPS = 3


EPSILON = 1e-06


def shifted(block, axis, distance):
    devices = range(lax.axis_size(axis))
    route = [((i - distance) % len(devices), i) for i in devices]
    return lax.ppermute(block, axis, route)


def contract_last(left, right):
    return lax.dot_general(
        left, right, (((1,), (1,)), ((), ())), preferred_element_type=jnp.float32
    )


def contract_first(left, right):
    return lax.dot_general(
        left, right, (((0,), (0,)), ((), ())), preferred_element_type=jnp.float32
    )


def on_device(x_in, grad_out, gain, w_val, w_out, filt, tail, micro_index):
    x_rows = x_in[0]
    cot_rows = grad_out[0]
    gain_row = gain[0]
    val_weight = w_val[0]
    out_weight = w_out[0]
    filters = filt[0]
    tail_rows = tail[0]
    has_tail = micro_index[0] > 0
    x_float = x_rows.astype(jnp.float32)
    inv_rms = lax.rsqrt(jnp.mean(x_float * x_float, axis=-1, keepdims=True) + EPSILON)
    normed = (x_float * inv_rms * gain_row).astype(jnp.bfloat16)
    normed_all = lax.all_gather(normed, "tensor", axis=0, tiled=True)
    seq_len = normed_all.shape[0]
    values = contract_last(normed_all, val_weight).astype(jnp.bfloat16)
    lead_rows = jnp.where(has_tail, tail_rows, jnp.zeros_like(tail_rows))
    extended = jnp.concatenate([lead_rows, values], axis=0).astype(jnp.float32)
    conv_out = filters[0] * extended[TAPS - 1 : TAPS - 1 + seq_len]
    for tap in range(1, TAPS):
        conv_out = conv_out + filters[tap] * extended[TAPS - 1 - tap : TAPS - 1 - tap + seq_len]
    gate_sig = jax.nn.sigmoid(conv_out)
    gated = (conv_out * gate_sig).astype(jnp.bfloat16)
    grad_gated = contract_last(lax.all_gather(cot_rows, "tensor", axis=0, tiled=True), out_weight)
    grad_wo = contract_first(gated, lax.all_gather(cot_rows, "tensor", axis=0, tiled=True))
    grad_conv = grad_gated * gate_sig * (1.0 + conv_out * (1.0 - gate_sig))
    grad_filter = jnp.stack(
        [
            jnp.sum(grad_conv * extended[TAPS - 1 - tap : TAPS - 1 - tap + seq_len], axis=0)
            for tap in range(TAPS)
        ]
    )
    padded = jnp.pad(grad_conv, ((TAPS - 1, TAPS - 1), (0, 0)))
    grad_ext = filters[0] * padded[0 : seq_len + TAPS - 1]
    for tap in range(1, TAPS):
        grad_ext = grad_ext + filters[tap] * padded[tap : tap + seq_len + TAPS - 1]
    grad_values = grad_ext[TAPS - 1 :].astype(jnp.bfloat16)
    grad_tail = jnp.where(has_tail, grad_ext[: TAPS - 1], jnp.zeros_like(grad_ext[: TAPS - 1]))
    grad_wv = contract_first(grad_values, normed_all)
    grad_normed = lax.psum_scatter(
        jnp.dot(grad_values, val_weight, preferred_element_type=jnp.float32).astype(jnp.bfloat16),
        "tensor",
        scatter_dimension=0,
        tiled=True,
    ).astype(jnp.float32)
    gain_term = jnp.sum(grad_normed * x_float * inv_rms, axis=0)
    grad_gain = lax.psum(gain_term, "tensor")
    scaled = gain_row * grad_normed
    grad_local = (
        cot_rows.astype(jnp.float32)
        + inv_rms * scaled
        - x_float * inv_rms**3 * jnp.mean(scaled * x_float, axis=-1, keepdims=True)
    )
    received = shifted(grad_local.astype(jnp.bfloat16), "section", -1)
    return (
        received[None],
        grad_wv.astype(jnp.bfloat16)[None],
        grad_wo.astype(jnp.bfloat16)[None],
        grad_filter[None],
        grad_tail[None],
        grad_gain[None],
    )


def solution(mesh):
    placed = (
        P("section", "tensor", None),
        P("section", "tensor", None),
        P("section", None),
        P("section", "tensor", None),
        P("section", "tensor", None),
        P("section", None, "tensor"),
        P("section", None, "tensor"),
        P("section"),
    )
    return jax.shard_map(
        on_device,
        mesh=mesh,
        in_specs=placed,
        out_specs=(
            P("section", "tensor", None),
            P("section", "tensor", None),
            P("section", "tensor", None),
            P("section", None, "tensor"),
            P("section", None, "tensor"),
            P("section", None),
        ),
        check_vma=False,
    )
```

profile of v0, /device:TPU:0, one launch (start us, length us, event | category | flops | bytes accessed | tf_op | source)
XLA Modules:
  0.0 214.0 jit_solution(14526826836390493479)
XLA Ops:
  7.2 0.0 all-gather.4.cloned.1.call-start
  7.2 1.2 fusion.26
  8.5 2.0 fusion.28
  10.5 0.0 all-gather.4.cloned.1.call-update
  10.5 0.0 all-gather.6.cloned.1.call-start
  10.6 0.7 all-gather.6.cloned.1.call-update
  11.3 0.0 reduce-scatter.2.cloned.1.call-start
  12.0 0.7 fusion.35
  12.7 0.7 fusion.37
  13.4 47.1 %all-gather.4.cloned.1.call-done = bf16[512,4096]{1,0:T(8,128)(2,1)} async-done(((bf16[64,4096]{1,0:T(8,128)(2,1)}), bf16[512,4096]{1,0:T(8,128)(2,1)}) %all-gather.4.cloned.1.call-update) | async-done | bytes 4194320 | tf_op jit(solution)/shard_map/all_gather | solution.py:42
  60.5 5.8 %fusion.19 = bf16[512,512]{1,0:T(8,128)(2,1)S(1)} fusion(bf16[512,4096]{1,0:T(8,128)(2,1)} %all-gather.4.cloned.1.call-done, bf16[1,512,4096]{2,1,0:T(8,128)(2,1)} %param.11), kind=kOutput, calls=%fused_computation.20 | convolution fusion | flops 2147745792 | bytes 8912896 | tf_op jit(solution)/shard_map/dot_general | solution.py:19
  66.4 0.2 maximum_convert_fusion
  66.5 0.3 multiply_add_fusion.1
  66.8 41.2 %all-gather.6.cloned.1.call-done = bf16[1,512,4096]{2,1,0:T(8,128)(2,1)} async-done(((bf16[1,64,4096]{2,1,0:T(8,128)(2,1)}), bf16[1,512,4096]{2,1,0:T(8,128)(2,1)}) %all-gather.6.cloned.1.call-update) | async-done | bytes 4194320 | tf_op jit(solution)/shard_map/all_gather | solution.py:52
  108.0 0.0 copy-start.3
  108.0 6.5 %multiply_reduce_fusion.2 = (f32[512]{0:T(512)S(1)}, f32[512]{0:T(512)S(1)}, f32[512]{0:T(512)S(1)}, f32[512,512]{1,0:T(8,128)S(1)}) fusion(f32[514,512]{1,0:T(8,128)S(1)} %maximum_convert_fusion, f32[512,512]{1,0:T(8,128)S(1)} %multiply_add_fusion.1, bf16[1,512,4096]{2,1,0:T(8,128)(2,1)} %param.12, bf16[1,512,4096]{2,1,0:T(8,128)(2,1)} %all-gather.6.cloned.1.call-done), kind=kOutput, calls=%fused_computation.36 | convolution fusion | flops 2151152128 | bytes 13637632 | tf_op jit(solution)/shard_map/dot_general | solution.py:19
  114.5 0.3 multiply_add_fusion
  114.8 0.0 copy-done.3
  114.8 4.4 %convolution_convert_fusion.2 = bf16[512,4096]{1,0:T(8,128)(2,1)} fusion(bf16[1,512,4096]{2,1,0:T(8,128)(2,1)S(1)} %copy-done.3, f32[514,512]{1,0:T(8,128)S(1)} %multiply_add_fusion), kind=kOutput, calls=%fused_computation.2 | convolution fusion | flops 2149580800 | bytes 8912896 | tf_op jit(solution)/shard_map/dot_general | solution.py:69
  119.2 0.0 reduce-scatter.2.cloned.1.call-update
  119.3 0.6 broadcast_in_dim.30
  119.9 0.6 fusion.34
  120.5 0.0 copy-start
  120.5 0.0 copy-start.2
  120.5 0.0 copy-start.1
  120.5 6.7 %fusion.1 = bf16[1,512,4096]{2,1,0:T(8,128)(2,1)} fusion(bf16[1,512,4096]{2,1,0:T(8,128)(2,1)} %all-gather.6.cloned.1.call-done, f32[512,512]{1,0:T(8,128)S(1)} %multiply_add_fusion.1), kind=kOutput, calls=%fused_computation.4 | convolution fusion | flops 2150891520 | bytes 9437184 | tf_op jit(solution)/shard_map/dot_general | solution.py:25
  127.2 41.0 %reduce-scatter.2.cloned.1.call-done = bf16[64,4096]{1,0:T(8,128)(2,1)} async-done(((bf16[512,4096]{1,0:T(8,128)(2,1)}), bf16[64,4096]{1,0:T(8,128)(2,1)}) %reduce-scatter.2.cloned.1.call-update) | async-done | bytes 524304 | tf_op jit(solution)/shard_map/reduce_scatter | solution.py:68
  168.1 0.0 copy-done
  168.1 0.0 copy-done.2
  168.1 1.4 fusion.32
  169.6 0.0 copy-done.1
  169.6 1.4 fusion.25
  171.0 2.6 %collective-permute-start = (bf16[64,4096]{1,0:T(8,128)(2,1)S(1)}, bf16[64,4096]{1,0:T(8,128)(2,1)S(1)}, u32[]{:S(2)}, u32[]{:S(2)}) collective-permute-start(bf16[64,4096]{1,0:T(8,128)(2,1)S(1)} %fusion.25), channel_id=1, source_target_pairs={{8,0},{16,8},{24,16},{0,24},{9,1},{17,9},{25,17},{1,25},{10,2},{18... | collective-permute-start | bytes 1572872 | tf_op jit(solution)/shard_map/ppermute | solution.py:15
  173.6 6.6 %fusion = bf16[1,512,4096]{2,1,0:T(8,128)(2,1)} fusion(bf16[512,4096]{1,0:T(8,128)(2,1)} %all-gather.4.cloned.1.call-done, f32[514,512]{1,0:T(8,128)S(1)} %multiply_add_fusion), kind=kOutput, calls=%fused_computation.3 | convolution fusion | flops 2149580800 | bytes 8912896 | tf_op jit(solution)/shard_map/dot_general | solution.py:25
  180.2 26.5 %psum.7 = f32[1,4096]{1,0:T(1,128)} all-reduce(f32[1,4096]{1,0:T(1,128)S(1)} %bitcast.61), channel_id=1, replica_groups=mesh['section'=4,'tensor'=8] {'tensor'}, use_global_device_ids=true, to_apply=%region_7.8 | all-reduce | flops 4096 | bytes 32768 | tf_op jit(solution)/shard_map/psum | solution.py:75
  206.7 0.0 collective-permute-done
  206.7 0.8 copy.16
  (3 shorter events, 0.0 us)
Async XLA Ops:
  7.2 53.4 %all-gather.4.cloned.1.call-start = ((), (), s32[]{:S(2)}) async-start(), calls=%async_computation.1 | async-start | bytes 4718592 | tf_op jit(solution)/shard_map/all_gather | solution.py:42
  10.5 97.5 %all-gather.6.cloned.1.call-start = ((), (), s32[]{:S(2)}) async-start(), calls=%async_computation.3 | async-start | bytes 4718592 | tf_op jit(solution)/shard_map/all_gather | solution.py:52
  11.3 156.8 %reduce-scatter.2.cloned.1.call-start = ((), (), s32[]{:S(2)}) async-start(), calls=%async_computation.2 | async-start | bytes 4718592 | tf_op jit(solution)/shard_map/reduce_scatter | solution.py:68
  108.0 6.8 %copy-start.3 = (bf16[1,512,4096]{2,1,0:T(8,128)(2,1)S(1)}, bf16[1,512,4096]{2,1,0:T(8,128)(2,1)}, u32[]{:S(2)}) copy-start(bf16[1,512,4096]{2,1,0:T(8,128)(2,1)} %param.11) | copy-start | bytes 12582916
  120.5 47.7 %copy-start = (bf16[1,64,4096]{2,1,0:T(8,128)(2,1)S(1)}, bf16[1,64,4096]{2,1,0:T(8,128)(2,1)}, u32[]{:S(2)}) copy-start(bf16[1,64,4096]{2,1,0:T(8,128)(2,1)} %param.8) | copy-start | bytes 1572868
  120.5 47.7 %copy-start.2 = (f32[1,4096]{1,0:T(1,128)S(1)}, f32[1,4096]{1,0:T(1,128)}, u32[]{:S(2)}) copy-start(f32[1,4096]{1,0:T(1,128)} %param.10) | copy-start | bytes 49156
  120.5 49.1 %copy-start.1 = (bf16[1,64,4096]{2,1,0:T(8,128)(2,1)S(1)}, bf16[1,64,4096]{2,1,0:T(8,128)(2,1)}, u32[]{:S(2)}) copy-start(bf16[1,64,4096]{2,1,0:T(8,128)(2,1)} %param.9) | copy-start | bytes 1572868
  171.0 35.7 %collective-permute-start = (bf16[64,4096]{1,0:T(8,128)(2,1)S(1)}, bf16[64,4096]{1,0:T(8,128)(2,1)S(1)}, u32[]{:S(2)}, u32[]{:S(2)}) collective-permute-start(bf16[64,4096]{1,0:T(8,128)(2,1)S(1)} %fusion.25), channel_id=1, source_target_pairs={{8,0},{16,8},{24,16},{0,24},{9,1},{17,9},{25,17},{1,25},{10,2},{18... | collective-permute-start | bytes 1572872 | tf_op jit(solution)/shard_map/ppermute | solution.py:15
Sparse Core Ops, SparseCore 0:
  10.7 49.8 all-gather.3
  62.1 45.8 all-gather.5
  119.4 48.7 reduce-scatter.1
where the time goes:
time: 214 us
  waiting for transfers between devices  130 us (61%)
  matrix products  29.9 us (14%)
  blocking collectives  26.5 us (12%)
  between operations  14.5 us (7%)
  other arithmetic  8.25 us (4%)
  starting transfers between devices  2.74 us (1%)
    all_gather x1, waiting for transfers between devices, on_device(): normed_all = lax.all_gather(normed, 'tensor', axis=0, tiled=True)  47.1 us
    all_gather x1, waiting for transfers between devices, on_device(): lax.all_gather(cot_rows, 'tensor', axis=0, tiled=True)  41.2 us
    reduce_scatter x1, waiting for transfers between devices, on_device(): lax.psum_scatter(jnp.dot(grad_values, val_weight, preferred_element_type=...  41 us
    psum x1, blocking collectives, on_device(): grad_gain = lax.psum(gain_term, 'tensor')  26.5 us
    dot_general x2, matrix products, contract_first(): lax.dot_general(left, right, (((0,), (0,)), ((), ())), preferred_element_...  13.3 us
    dot_general x2, matrix products, contract_last(): lax.dot_general(left, right, (((1,), (1,)), ((), ())), preferred_element_...  12.3 us
    dot_general x1, matrix products, on_device(): jnp.dot(grad_values, val_weight, preferred_element_type=jnp.float32)  4.38 us
  transfers between devices with their start and end apart: 4, of which 3 were waited for; matrix products, arithmetic and copies ran while one was open for 10% of the time, Pallas kernels for 0%

commit v1 on v0

v1 whole, which is shorter than its diff:
```python
import functools

import jax
import jax.numpy as jnp
from jax import lax
from jax.experimental import pallas as pl
from jax.experimental.pallas import tpu as pltpu
from jax.sharding import PartitionSpec as P

TAPS = 3
EPSILON = 1e-06
MESH = pl.DeviceIdType.MESH
F32 = jnp.float32
BF16 = jnp.bfloat16


def dot_nt(left, right):
    return lax.dot_general(left, right, (((1,), (1,)), ((), ())), preferred_element_type=F32)


def dot_nn(left, right):
    return lax.dot_general(left, right, (((1,), (0,)), ((), ())), preferred_element_type=F32)


def kernel(
    n, sections, cuts, col_tile,
    x_ref, cot_ref, gain_ref, wv_hbm, wo_hbm, filt_ref, tail_ref, micro_ref,
    gin_out, gwv_out, gwo_out, gfilt_out, gtail_out, ggain_out,
    nrm, got, wv, wo, vals, gg, gat_t, gv, gv_t, gwo, gwv, part, sib, inc, outg, local, gparts, own,
    ag_send, ag_recv, own_sem, sib_send, sib_recv, line_send, line_recv,
    gain_send, gain_recv, load_sem, store_sem, shift_send, shift_recv,
):
    chips = n // 2
    rows = x_ref.shape[1]
    width = x_ref.shape[2]
    tokens = rows * n
    channels = wv.shape[0]
    wide = width // cuts
    me = lax.axis_index("tensor")
    sec = lax.axis_index("section")
    z = me // 2
    c = me % 2
    other = z * 2 + (1 - c)
    sec_prev = lax.rem(sec + sections - 1, sections)
    sec_next = lax.rem(sec + 1, sections)

    def rows_of(d):
        return pl.ds(pl.multiple_of(d * rows, rows), rows)

    load_cot = pltpu.make_async_copy(cot_ref.at[0], got.at[rows_of(me)], load_sem.at[0])
    load_wv = pltpu.make_async_copy(wv_hbm.at[0], wv, load_sem.at[1])
    load_wo = pltpu.make_async_copy(wo_hbm.at[0], wo, load_sem.at[2])
    load_cot.start()
    load_wo.start()
    load_wv.start()

    barrier = pltpu.get_barrier_semaphore()

    def greet(k, _):
        pl.semaphore_signal(
            barrier, inc=1, device_id={"tensor": lax.rem(me + k, n)}, device_id_type=MESH
        )
        return 0

    lax.fori_loop(1, n, greet, 0)
    pl.semaphore_signal(barrier, inc=1, device_id={"section": sec_prev}, device_id_type=MESH)
    pl.semaphore_signal(barrier, inc=1, device_id={"section": sec_next}, device_id_type=MESH)

    x_float = x_ref[0].astype(F32)
    inv_rms = lax.rsqrt(jnp.mean(x_float * x_float, axis=-1, keepdims=True) + EPSILON)
    nrm[rows_of(me), :] = (x_float * inv_rms * gain_ref[...]).astype(BF16)
    pl.semaphore_wait(barrier, n + 1)

    gathered = (got, nrm)

    def ag_copy(a, d, way, target):
        buf = gathered[a]
        return pltpu.make_async_remote_copy(
            src_ref=buf.at[rows_of(d)],
            dst_ref=buf.at[rows_of(d)],
            send_sem=ag_send.at[way, a, d],
            recv_sem=ag_recv.at[a, d],
            device_id={"tensor": target},
            device_id_type=MESH,
        )

    def ag_each(a, b, act):
        d = 2 * b + c

        @pl.when((b <= z) & (z < chips - 1))
        def _():
            act(ag_copy(a, d, 0, me + 2))

        @pl.when((b >= z) & (z > 0))
        def _():
            act(ag_copy(a, d, 1, me - 2))

        act(ag_copy(a, d, 2, other))

    def start(copy):
        copy.start()

    load_cot.wait()
    ag_each(0, z, start)
    ag_each(1, z, start)
    load_wo.wait()
    load_wv.wait()

    def project(b):
        d = 2 * b + (1 - c)
        pair = pl.ds(pl.multiple_of(b * 2 * rows, 2 * rows), 2 * rows)
        ag_copy(0, d, 2, other).wait_recv()
        gg[pair, :] = dot_nt(got[pair, :], wo[...])
        ag_copy(1, d, 2, other).wait_recv()
        vals[pair, :] = dot_nt(nrm[pair, :], wv[...]).astype(BF16).astype(F32)

    def project_at(s):
        @pl.when(z - s >= 0)
        def _():
            project(z - s)

        @pl.when(z + s < chips)
        def _():
            project(z + s)

    def ag_step(s, _):
        for a in range(2):

            @pl.when(z - s >= 0)
            def _():
                ag_copy(a, 2 * (z - s) + c, 0, me).wait_recv()
                ag_each(a, z - s, start)

            @pl.when(z + s < chips)
            def _():
                ag_copy(a, 2 * (z + s) + c, 1, me).wait_recv()
                ag_each(a, z + s, start)

            if a == 0:

                @pl.when(s == 1)
                def _():
                    project(z)

                @pl.when(s > 1)
                def _():
                    project_at(s - 1)

        return 0

    lax.fori_loop(1, chips, ag_step, 0)
    project_at(chips - 1)

    has_tail = (micro_ref[0] > 0).astype(F32)

    def strip(i, _):
        cs = pl.ds(pl.multiple_of(i * 128, 128), 128)
        v = vals[:, cs]
        f = [filt_ref[0, k : k + 1, cs] for k in range(TAPS)]
        lead = tail_ref[0, :, cs].astype(F32) * has_tail
        row = lax.broadcasted_iota(jnp.int32, (tokens, 128), 0)
        v1 = jnp.where(row == 0, lead[1:2], pltpu.roll(v, 1, 0))
        v2 = jnp.where(row == 0, lead[0:1], jnp.where(row == 1, lead[1:2], pltpu.roll(v, 2, 0)))
        conv = f[0] * v + f[1] * v1 + f[2] * v2
        sig = jax.nn.sigmoid(conv)
        gat_t[cs, :] = (conv * sig).T.astype(BF16)
        gc = gg[:, cs] * sig * (1.0 + conv * (1.0 - sig))
        gfilt_out[0, 0:1, cs] = jnp.sum(gc * v, axis=0, keepdims=True)
        gfilt_out[0, 1:2, cs] = jnp.sum(gc * v1, axis=0, keepdims=True)
        gfilt_out[0, 2:3, cs] = jnp.sum(gc * v2, axis=0, keepdims=True)
        gc1 = jnp.where(row == tokens - 1, 0.0, pltpu.roll(gc, tokens - 1, 0))
        gc2 = jnp.where(row >= tokens - 2, 0.0, pltpu.roll(gc, tokens - 2, 0))
        grad_values = f[0] * gc + f[1] * gc1 + f[2] * gc2
        gv[:, cs] = grad_values.astype(BF16)
        gv_t[cs, :] = grad_values.T.astype(BF16)
        gtail_out[0, 0:1, cs] = f[2] * gc[0:1] * has_tail
        gtail_out[0, 1:2, cs] = (f[1] * gc[0:1] + f[2] * gc[1:2]) * has_tail
        return 0

    lax.fori_loop(0, channels // 128, strip, 0)

    def sib_copy(q, b):
        return pltpu.make_async_remote_copy(
            src_ref=part.at[q, rows_of(2 * b + (1 - c))],
            dst_ref=sib.at[q, b],
            send_sem=sib_send.at[q, b],
            recv_sem=sib_recv.at[q, b],
            device_id={"tensor": other},
            device_id_type=MESH,
        )

    def line_copy(q, b, slot, target):
        return pltpu.make_async_remote_copy(
            src_ref=outg.at[q, b],
            dst_ref=inc.at[q, slot],
            send_sem=line_send.at[q, b],
            recv_sem=line_recv.at[q, slot],
            device_id={"tensor": target},
            device_id_type=MESH,
        )

    def share(q, _):
        cols = pl.ds(pl.multiple_of(q * wide, wide), wide)
        part[q] = dot_nn(gv[...], wv[:, cols]).astype(BF16)

        def send(b, _):
            sib_copy(q, b).start()
            return 0

        lax.fori_loop(0, chips, send, 0)
        return 0

    lax.fori_loop(0, cuts, share, 0)

    def chip_sum(q, b):
        sib_copy(q, b).wait_recv()
        return part[q, rows_of(2 * b + c), :].astype(F32) + sib[q, b].astype(F32)

    def rs_step(s):
        right = chips - 1 - s + z
        left = s - (chips - 1 - z)

        def piece(q, _):
            @pl.when((s >= z) & (right > z))
            def _():
                total = chip_sum(q, right)
                outg[q, right] = total.astype(BF16)

                @pl.when(z > 0)
                def _():
                    line_copy(q, right, right, me).wait_recv()
                    outg[q, right] = (total + inc[q, right].astype(F32)).astype(BF16)

                slot = jnp.where(right == z + 1, chips, right)
                line_copy(q, right, slot, me + 2).start()

            @pl.when((left >= 0) & (left < z))
            def _():
                total = chip_sum(q, left)
                outg[q, left] = total.astype(BF16)

                @pl.when(z < chips - 1)
                def _():
                    line_copy(q, left, left, me).wait_recv()
                    outg[q, left] = (total + inc[q, left].astype(F32)).astype(BF16)

                line_copy(q, left, left, me - 2).start()

            return 0

        lax.fori_loop(0, cuts, piece, 0)

    def gain_copy(k):
        return pltpu.make_async_remote_copy(
            src_ref=gparts.at[me],
            dst_ref=gparts.at[me],
            send_sem=gain_send.at[k],
            recv_sem=gain_recv.at[me],
            device_id={"tensor": lax.rem(me + k, n)},
            device_id_type=MESH,
        )

    def gain_arrival(k):
        d = lax.rem(me + k, n)
        return pltpu.make_async_remote_copy(
            src_ref=gparts.at[d],
            dst_ref=gparts.at[d],
            send_sem=gain_send.at[k],
            recv_sem=gain_recv.at[d],
            device_id={"tensor": d},
            device_id_type=MESH,
        )

    store_wo = pltpu.make_async_copy(gwo, gwo_out.at[0], store_sem.at[0])
    store_wv = pltpu.make_async_copy(gwv, gwv_out.at[0], store_sem.at[1])

    def weights_out():
        def tile(j, _):
            cols = pl.ds(pl.multiple_of(j * col_tile, col_tile), col_tile)
            gwo[:, cols] = dot_nn(gat_t[...], got[:, cols]).astype(BF16)
            return 0

        lax.fori_loop(0, width // col_tile, tile, 0)
        store_wo.start()

    def weights_val():
        def tile(j, _):
            cols = pl.ds(pl.multiple_of(j * col_tile, col_tile), col_tile)
            grad = dot_nn(gv_t[...], nrm[:, cols])
            gwv[:, cols] = grad.astype(BF16)
            own[:, cols] = (
                jnp.sum(grad * wv[:, cols].astype(F32), axis=0, keepdims=True) / gain_ref[:, cols]
            )
            return 0

        lax.fori_loop(0, width // col_tile, tile, 0)
        store_wv.start()
        gparts[me] = own[...]

        def send(k, _):
            gain_copy(k).start()
            return 0

        lax.fori_loop(1, n, send, 0)

    rs_step(0)
    weights_out()
    rs_step(1)
    weights_val()

    def rest(s, _):
        rs_step(s)
        return 0

    lax.fori_loop(2, chips - 1, rest, 0)

    def mine(q, dots):
        cols = pl.ds(pl.multiple_of(q * wide, wide), wide)
        local[:, cols] = chip_sum(q, z)

        @pl.when(z > 0)
        def _():
            line_copy(q, z, chips, me).wait_recv()
            local[:, cols] += inc[q, chips].astype(F32)

        @pl.when(z < chips - 1)
        def _():
            line_copy(q, z, z, me).wait_recv()
            local[:, cols] += inc[q, z].astype(F32)

        scaled = local[:, cols] * gain_ref[:, cols]
        local[:, cols] = scaled
        return dots + jnp.sum(scaled * x_ref[0, :, cols].astype(F32), axis=-1, keepdims=True)

    dots = lax.fori_loop(0, cuts, mine, jnp.zeros((rows, 1), F32))
    factor = inv_rms**3 * (dots / width)
    outgoing = nrm.at[rows_of(me)]

    def ag_drain(b, _):
        for a in range(2):
            ag_each(a, b, lambda copy: copy.wait_send())
        return 0

    lax.fori_loop(0, chips, ag_drain, 0)
    outgoing[...] = (
        cot_ref[0].astype(F32) + inv_rms * local[...] - x_ref[0].astype(F32) * factor
    ).astype(BF16)
    shift = pltpu.make_async_remote_copy(
        src_ref=outgoing,
        dst_ref=gin_out.at[0],
        send_sem=shift_send,
        recv_sem=shift_recv,
        device_id={"section": sec_prev},
        device_id_type=MESH,
    )
    shift.start()

    def gain_wait(k, _):
        gain_arrival(k).wait_recv()
        gain_copy(k).wait_send()
        return 0

    lax.fori_loop(1, n, gain_wait, 0)
    ggain_out[...] = jnp.sum(gparts[...], axis=0)

    def rs_drain(i, _):
        q, b = i // chips, i % chips
        sib_copy(q, b).wait_send()

        @pl.when(b != z)
        def _():
            line_copy(q, b, b, me).wait_send()

        return 0

    lax.fori_loop(0, cuts * chips, rs_drain, 0)
    store_wo.wait()
    store_wv.wait()
    shift.wait()


def on_device(n, sections, x_in, grad_out, gain, w_val, w_out, filt, tail, micro_index):
    _, rows, width = x_in.shape
    channels = w_val.shape[1]
    chips = n // 2
    tokens = rows * n
    cuts = 4
    wide = width // cuts
    vmem = pl.BlockSpec(memory_space=pltpu.VMEM)
    hbm = pl.BlockSpec(memory_space=pl.ANY)
    dma = pltpu.SemaphoreType.DMA
    return pl.pallas_call(
        functools.partial(kernel, n, sections, cuts, 512),
        out_shape=(
            jax.ShapeDtypeStruct(x_in.shape, BF16),
            jax.ShapeDtypeStruct(w_val.shape, BF16),
            jax.ShapeDtypeStruct(w_out.shape, BF16),
            jax.ShapeDtypeStruct(filt.shape, F32),
            jax.ShapeDtypeStruct(tail.shape, F32),
            jax.ShapeDtypeStruct(gain.shape, F32),
        ),
        in_specs=[vmem, vmem, vmem, hbm, hbm, vmem, vmem, pl.BlockSpec(memory_space=pltpu.SMEM)],
        out_specs=(hbm, hbm, hbm, vmem, vmem, vmem),
        scratch_shapes=[
            pltpu.VMEM((tokens, width), BF16),
            pltpu.VMEM((tokens, width), BF16),
            pltpu.VMEM((channels, width), BF16),
            pltpu.VMEM((channels, width), BF16),
            pltpu.VMEM((tokens, channels), F32),
            pltpu.VMEM((tokens, channels), F32),
            pltpu.VMEM((channels, tokens), BF16),
            pltpu.VMEM((tokens, channels), BF16),
            pltpu.VMEM((channels, tokens), BF16),
            pltpu.VMEM((channels, width), BF16),
            pltpu.VMEM((channels, width), BF16),
            pltpu.VMEM((cuts, tokens, wide), BF16),
            pltpu.VMEM((cuts, chips, rows, wide), BF16),
            pltpu.VMEM((cuts, chips + 1, rows, wide), BF16),
            pltpu.VMEM((cuts, chips, rows, wide), BF16),
            pltpu.VMEM((rows, width), F32),
            pltpu.VMEM((n, 1, width), F32),
            pltpu.VMEM((1, width), F32),
            dma((3, 2, n)),
            dma((2, n)),
            dma,
            dma((cuts, chips)),
            dma((cuts, chips)),
            dma((cuts, chips)),
            dma((cuts, chips + 1)),
            dma((n,)),
            dma((n,)),
            dma((3,)),
            dma((2,)),
            dma,
            dma,
        ],
        compiler_params=pltpu.CompilerParams(
            collective_id=0, has_side_effects=True, vmem_limit_bytes=60 * 2**20
        ),
    )(x_in, grad_out, gain, w_val, w_out, filt, tail, micro_index)


def solution(mesh):
    placed = (
        P("section", "tensor", None),
        P("section", "tensor", None),
        P("section", None),
        P("section", "tensor", None),
        P("section", "tensor", None),
        P("section", None, "tensor"),
        P("section", None, "tensor"),
        P("section"),
    )
    return jax.shard_map(
        functools.partial(on_device, mesh.shape["tensor"], mesh.shape["section"]),
        mesh=mesh,
        in_specs=placed,
        out_specs=(
            P("section", "tensor", None),
            P("section", "tensor", None),
            P("section", "tensor", None),
            P("section", None, "tensor"),
            P("section", None, "tensor"),
            P("section", None),
        ),
        check_vma=False,
    )
```

time: 214 us -> 149 us (0.70)
  the two profiles are of different devices: /device:TPU:0 before, /device:TPU:12 now
where the time goes in v1:
time: 149 us
  Pallas kernels  135 us (91%)
  local copies, waits for them, and re-layouts  12.5 us (8%)
    pallas_call x1, Pallas kernels, on_device(): pl.pallas_call(functools.partial(kernel, n, sections, cuts, 512), out_sha...  135 us
    unnamed x12, local copies, waits for them, and re-layouts  11.2 us

profile of v1, /device:TPU:12, one launch (start us, length us, event | category | flops | bytes accessed | tf_op | source)
XLA Modules:
  0.0 149.0 jit_solution(11287914941021491318)
XLA Ops:
  1.3 1.3 copy.14.filt_ref
  2.6 135.2 %shard_map.127 = (bf16[1,64,4096]{2,1,0:T(8,128)(2,1)}, bf16[1,512,4096]{2,1,0:T(8,128)(2,1)}, bf16[1,512,4096]{2,1,0:T(8,128)(2,1)}, f32[1,3,512]{2,1,0:T(4,128...) custom-call(bf16[1,64,4096]{2,1,0:T(8,128)(2,1)} %x_ref.1, bf16[1,64,4096]{2,1,0:T(8,128)(2,1)} %cot_ref.1, ...), custom_call_target="tpu_custom_call" | custom-call | tf_op jit(solution)/shard_map/pallas_call | solution.py:392
  137.8 1.3 copy.15
  139.1 1.9 %copy.22 = bf16[1,64,4096]{2,1,0:T(8,128)(2,1)} copy(bf16[1,64,4096]{2,1,0:T(8,128)(2,1)} %get-tuple-element.18) | data formatting | bytes 1048576
  140.9 0.0 copy-start
  140.9 4.8 %copy.23 = bf16[1,512,4096]{2,1,0:T(8,128)(2,1)} copy(bf16[1,512,4096]{2,1,0:T(8,128)(2,1)} %get-tuple-element.19) | data formatting | bytes 8388608
  145.8 0.0 copy-done
  145.8 0.0 copy-start.2
  145.8 0.0 copy-start.1
  145.8 2.0 %copy.24 = bf16[1,512,4096]{2,1,0:T(8,128)(2,1)} copy(bf16[1,512,4096]{2,1,0:T(8,128)(2,1)S(1)} %copy-done) | data formatting | bytes 8388608
  147.8 0.0 copy-done.2
  147.8 0.6 copy.25
  148.4 0.0 copy-done.1
  148.4 0.6 copy.26
Async XLA Ops:
  140.9 4.9 %copy-start = (bf16[1,512,4096]{2,1,0:T(8,128)(2,1)S(1)}, bf16[1,512,4096]{2,1,0:T(8,128)(2,1)}, u32[]{:S(2)}) copy-start(bf16[1,512,4096]{2,1,0:T(8,128)(2,1)} %get-tuple-element.20) | copy-start | bytes 12582916
  145.8 2.0 %copy-start.2 = (f32[1,2,512]{2,1,0:T(2,128)S(1)}, f32[1,2,512]{2,1,0:T(2,128)}, u32[]{:S(2)}) copy-start(f32[1,2,512]{2,1,0:T(2,128)} %get-tuple-element.22) | copy-start | bytes 12292
  145.8 2.6 %copy-start.1 = (f32[1,4096]{1,0:T(1,128)S(1)}, f32[1,4096]{1,0:T(1,128)}, u32[]{:S(2)}) copy-start(f32[1,4096]{1,0:T(1,128)} %get-tuple-element.23) | copy-start | bytes 49156

commit v2 on v0

v2 whole, which is shorter than its diff:
```python
import functools

import jax
import jax.numpy as jnp
from jax import lax
from jax.experimental import pallas as pl
from jax.experimental.pallas import tpu as pltpu
from jax.sharding import PartitionSpec as P

TAPS = 3
EPSILON = 1e-06
MESH = pl.DeviceIdType.MESH
F32 = jnp.float32
BF16 = jnp.bfloat16


def dot_nt(left, right):
    return lax.dot_general(left, right, (((1,), (1,)), ((), ())), preferred_element_type=F32)


def dot_nn(left, right):
    return lax.dot_general(left, right, (((1,), (0,)), ((), ())), preferred_element_type=F32)


def kernel(
    n, col_tile,
    x_ref, cot_ref, gain_ref, wv_hbm, wo_hbm, filt_ref, tail_ref, micro_ref,
    gloc_out, nrm_out, got_out, gat_t, gv_t, gfilt_out, gtail_out, ggain_out,
    nrm, got, wv, wo, vals, gg, gat, gv, part, sib, inc, outg, gparts, own,
    ag_send, ag_recv, sib_send, sib_recv, line_send, line_recv,
    gain_send, gain_recv, load_sem, store_sem,
):
    chips = n // 2
    rows = x_ref.shape[1]
    width = x_ref.shape[2]
    tokens = rows * n
    channels = wv.shape[0]
    height = 16
    cuts = rows // height
    hop = 2
    last = chips - 1
    me = lax.axis_index("tensor")
    z = me // 2
    c = me % 2
    other = z * 2 + (1 - c)

    def rows_of(d):
        return pl.ds(pl.multiple_of(d * rows, rows), rows)

    def piece_of(q):
        return pl.ds(pl.multiple_of(q * height, height), height)

    load_cot = pltpu.make_async_copy(cot_ref.at[0], got.at[rows_of(me)], load_sem.at[0])
    load_wv = pltpu.make_async_copy(wv_hbm.at[0], wv, load_sem.at[1])
    load_wo = pltpu.make_async_copy(wo_hbm.at[0], wo, load_sem.at[2])
    load_cot.start()
    load_wo.start()
    load_wv.start()

    barrier = pltpu.get_barrier_semaphore()

    def greet(k, _):
        pl.semaphore_signal(
            barrier, inc=1, device_id={"tensor": lax.rem(me + k, n)}, device_id_type=MESH
        )
        return 0

    lax.fori_loop(1, n, greet, 0)

    x_float = x_ref[0].astype(F32)
    inv_rms = lax.rsqrt(jnp.mean(x_float * x_float, axis=-1, keepdims=True) + EPSILON)
    nrm[rows_of(me), :] = (x_float * inv_rms * gain_ref[...]).astype(BF16)

    has_tail = (micro_ref[0] > 0).astype(F32)
    vals[0:8, :] = jnp.zeros((8, channels), F32)
    vals[6:8, :] = tail_ref[0].astype(F32) * has_tail
    vals[tokens + 8 : tokens + 16, :] = jnp.zeros((8, channels), F32)
    gg[tokens : tokens + 8, :] = jnp.zeros((8, channels), F32)
    gfilt_out[...] = jnp.zeros_like(gfilt_out)
    pl.semaphore_wait(barrier, n - 1)

    gathered = (got, nrm)

    def ag_copy(a, d, way, target):
        buf = gathered[a]
        return pltpu.make_async_remote_copy(
            src_ref=buf.at[rows_of(d)],
            dst_ref=buf.at[rows_of(d)],
            send_sem=ag_send.at[way, a, d],
            recv_sem=ag_recv.at[a, d],
            device_id={"tensor": target},
            device_id_type=MESH,
        )

    def ag_each(a, b, act):
        d = 2 * b + c

        @pl.when((b <= z) & (z < last))
        def _():
            act(ag_copy(a, d, 0, me + 2))

        @pl.when((b >= z) & (z > 0))
        def _():
            act(ag_copy(a, d, 1, me - 2))

        act(ag_copy(a, d, 2, other))

    def start(copy):
        copy.start()

    load_cot.wait()
    ag_each(0, z, start)
    ag_each(1, z, start)
    load_wo.wait()
    load_wv.wait()

    def project(a, b):
        ag_copy(a, 2 * b + (1 - c), 2, other).wait_recv()
        first = pl.multiple_of(b * 2 * rows, 2 * rows)
        pair = pl.ds(first, 2 * rows)
        if a == 0:
            gg[pair, :] = dot_nt(got[pair, :], wo[...])
        else:
            vals[pl.ds(pl.multiple_of(first + 8, 8), 2 * rows), :] = (
                dot_nt(nrm[pair, :], wv[...]).astype(BF16).astype(F32)
            )

    def project_at(a, s):
        @pl.when(z - s >= 0)
        def _():
            project(a, z - s)

        @pl.when((z + s < chips) & (s > 0))
        def _():
            project(a, z + s)

    def sib_copy(b):
        return pltpu.make_async_remote_copy(
            src_ref=part.at[rows_of(2 * b + (1 - c))],
            dst_ref=sib.at[b],
            send_sem=sib_send.at[b],
            recv_sem=sib_recv.at[b],
            device_id={"tensor": other},
            device_id_type=MESH,
        )

    def share(d, _):
        first = pl.multiple_of(d * rows, rows)

        def strip(i, _):
            cs = pl.ds(pl.multiple_of(i * 128, 128), 128)
            window = vals[pl.ds(first, rows + 16), cs]
            f = [filt_ref[0, k : k + 1, cs] for k in range(TAPS)]
            v = window[8:]
            v1 = pltpu.roll(window, 1, 0)[8:]
            v2 = pltpu.roll(window, 2, 0)[8:]
            conv = f[0] * v + f[1] * v1 + f[2] * v2
            sig = jax.nn.sigmoid(conv)
            gat[rows_of(d), cs] = (conv * sig)[:rows].astype(BF16)
            gc = gg[pl.ds(first, rows + 8), cs] * sig * (1.0 + conv * (1.0 - sig))
            gc1 = pltpu.roll(gc, rows + 7, 0)[:rows]
            gc2 = pltpu.roll(gc, rows + 6, 0)[:rows]
            here = gc[:rows]
            for k, shifted in enumerate((v, v1, v2)):
                gfilt_out[0, k : k + 1, cs] += jnp.sum(here * shifted[:rows], axis=0, keepdims=True)
            gv[rows_of(d), cs] = (f[0] * here + f[1] * gc1 + f[2] * gc2).astype(BF16)

            @pl.when(d == 0)
            def _():
                gtail_out[0, 0:1, cs] = f[2] * gc[0:1] * has_tail
                gtail_out[0, 1:2, cs] = (f[1] * gc[0:1] + f[2] * gc[1:2]) * has_tail

            return 0

        lax.fori_loop(0, channels // 128, strip, 0)

        def tile(j, _):
            cols = pl.ds(pl.multiple_of(j * col_tile, col_tile), col_tile)
            part[rows_of(d), cols] = dot_nn(gv[rows_of(d), :], wv[:, cols]).astype(BF16)
            return 0

        lax.fori_loop(0, width // col_tile, tile, 0)

        @pl.when(d % 2 != c)
        def _():
            sib_copy(d // 2).start()

        return 0

    def low_end(s):
        lo = z - s
        return jnp.where(lo > 0, 2 * lo + 1, 0)

    def high_end(s):
        hi = z + s
        return jnp.where(hi < last, 2 * hi + 1, n)

    def line_copy(q, b, slot, target):
        return pltpu.make_async_remote_copy(
            src_ref=outg.at[b, piece_of(q)],
            dst_ref=inc.at[slot, piece_of(q)],
            send_sem=line_send.at[q, b],
            recv_sem=line_recv.at[q, slot],
            device_id={"tensor": target},
            device_id_type=MESH,
        )

    def chip_sum(q, b):
        mine = pl.ds(pl.multiple_of((2 * b + c) * rows + q * height, height), height)
        return part[mine, :].astype(F32) + sib[b, piece_of(q), :].astype(F32)

    def forward(q, b, slot, target, upstream):
        @pl.when(q == 0)
        def _():
            sib_copy(b).wait_recv()

        @pl.when(upstream)
        def _():
            line_copy(q, b, b, me).wait_recv()
            outg[b, piece_of(q), :] = (
                chip_sum(q, b) + inc[b, piece_of(q), :].astype(F32)
            ).astype(BF16)

        @pl.when(jnp.logical_not(upstream))
        def _():
            outg[b, piece_of(q), :] = chip_sum(q, b).astype(BF16)

        line_copy(q, b, slot, target).start()

    def order(i, late):
        return jnp.where((late == 1) & (i >= last - 1), 2 * last - 1 - i, i)

    def right_at(t):
        u = t - hop * z
        b = order(u // cuts, c)

        @pl.when((u >= cuts) & (u < cuts * chips) & (b > z))
        def _():
            forward(u % cuts, b, jnp.where(b == z + 1, chips, b), me + 2, z > 0)

    def left_at(t):
        u = t - hop * (last - z)
        b = last - order(u // cuts, 1 - c)

        @pl.when((u >= cuts) & (u < cuts * chips) & (b < z))
        def _():
            forward(u % cuts, b, b, me - 2, z < last)

    def windows(s):
        def turn(q, _):
            right_at((s - c) * cuts + q)
            left_at((s - (1 - c)) * cuts + q)
            return 0

        lax.fori_loop(0, cuts, turn, 0)

    def shares(s, low, high):
        lax.fori_loop(low_end(s), low, share, 0)
        lax.fori_loop(high, high_end(s), share, 0)

    def gain_copy(k, d):
        return pltpu.make_async_remote_copy(
            src_ref=gparts.at[d],
            dst_ref=gparts.at[d],
            send_sem=gain_send.at[k],
            recv_sem=gain_recv.at[d],
            device_id={"tensor": lax.rem(me + k, n)},
            device_id_type=MESH,
        )

    store_nrm = pltpu.make_async_copy(nrm, nrm_out, store_sem.at[0])
    store_got = pltpu.make_async_copy(got, got_out, store_sem.at[1])

    def gain_part():
        store_nrm.start()
        store_got.start()

        def turned(i, _):
            cs = pl.ds(pl.multiple_of(i * 128, 128), 128)
            gat_t[cs, :] = gat[:, cs].astype(F32).T.astype(BF16)
            gv_t[cs, :] = gv[:, cs].astype(F32).T.astype(BF16)
            return 0

        lax.fori_loop(0, channels // 128, turned, 0)

        def tile(j, _):
            cols = pl.ds(pl.multiple_of(j * col_tile, col_tile), col_tile)
            grad = dot_nn(gv_t[...], nrm[:, cols])
            own[:, cols] = (
                jnp.sum(grad * wv[:, cols].astype(F32), axis=0, keepdims=True) / gain_ref[:, cols]
            )
            return 0

        lax.fori_loop(0, width // col_tile, tile, 0)
        gparts[me] = own[...]

        def send(k, _):
            gain_copy(k, me).start()
            return 0

        lax.fori_loop(1, n, send, 0)

    def process(s, low, high):
        project_at(1, s)
        shares(s, low, high)
        windows(s)

    inner = (z > 0) & (z < last)
    project_at(0, 0)
    process(0, 2 * z + 1, 2 * z + 1)

    def ag_step(s, _):
        for a in range(2):

            @pl.when(z - s >= 0)
            def _():
                ag_copy(a, 2 * (z - s) + c, 0, me).wait_recv()
                ag_each(a, z - s, start)

            @pl.when(z + s < chips)
            def _():
                ag_copy(a, 2 * (z + s) + c, 1, me).wait_recv()
                ag_each(a, z + s, start)

            if a == 0:
                project_at(0, s)

        process(s, low_end(s - 1), high_end(s - 1))

        @pl.when((s == last - 1) & inner)
        def _():
            gain_part()

        return 0

    lax.fori_loop(1, chips, ag_step, 0)

    def rest(t, _):
        right_at(t + (1 - c) * cuts)
        left_at(t + c * cuts)
        return 0

    lax.fori_loop(cuts * last, cuts * chips + hop * chips, rest, 0)

    @pl.when(jnp.logical_not(inner))
    def _():
        gain_part()

    sib_copy(z).wait_recv()

    def finish(q, _):
        @pl.when(z > 0)
        def _():
            line_copy(q, z, chips, me).wait_recv()

        @pl.when(z < last)
        def _():
            line_copy(q, z, z, me).wait_recv()

        from_left = jnp.where(z > 0, inc[chips, piece_of(q), :].astype(F32), 0.0)
        from_right = jnp.where(z < last, inc[z, piece_of(q), :].astype(F32), 0.0)
        scaled = (chip_sum(q, z) + from_left + from_right) * gain_ref[...]
        x_now = x_ref[0, piece_of(q), :].astype(F32)
        inv = lax.rsqrt(jnp.mean(x_now * x_now, axis=-1, keepdims=True) + EPSILON)
        dots = jnp.mean(scaled * x_now, axis=-1, keepdims=True)
        gloc_out[piece_of(q), :] = (
            cot_ref[0, piece_of(q), :].astype(F32) + inv * scaled - x_now * (inv**3 * dots)
        ).astype(BF16)
        return 0

    lax.fori_loop(0, cuts, finish, 0)

    def gain_wait(k, _):
        gain_copy(k, lax.rem(me + k, n)).wait_recv()
        gain_copy(k, me).wait_send()
        return 0

    lax.fori_loop(1, n, gain_wait, 0)
    ggain_out[...] = jnp.sum(gparts[...], axis=0)

    def ag_drain(b, _):
        for a in range(2):
            ag_each(a, b, lambda copy: copy.wait_send())
        sib_copy(b).wait_send()
        return 0

    lax.fori_loop(0, chips, ag_drain, 0)

    def line_drain(i, _):
        q, b = i // chips, i % chips

        @pl.when(b != z)
        def _():
            line_copy(q, b, b, me).wait_send()

        return 0

    lax.fori_loop(0, cuts * chips, line_drain, 0)
    store_nrm.wait()
    store_got.wait()


def on_device(n, sections, x_in, grad_out, gain, w_val, w_out, filt, tail, micro_index):
    _, rows, width = x_in.shape
    channels = w_val.shape[1]
    chips = n // 2
    tokens = rows * n
    cuts = rows // 16
    vmem = pl.BlockSpec(memory_space=pltpu.VMEM)
    hbm = pl.BlockSpec(memory_space=pl.ANY)
    dma = pltpu.SemaphoreType.DMA
    grad_local, normed, cot, gat_t, gv_t, grad_filter, grad_tail, grad_gain = pl.pallas_call(
        functools.partial(kernel, n, 512),
        out_shape=(
            jax.ShapeDtypeStruct((rows, width), BF16),
            jax.ShapeDtypeStruct((tokens, width), BF16),
            jax.ShapeDtypeStruct((tokens, width), BF16),
            jax.ShapeDtypeStruct((channels, tokens), BF16),
            jax.ShapeDtypeStruct((channels, tokens), BF16),
            jax.ShapeDtypeStruct(filt.shape, F32),
            jax.ShapeDtypeStruct(tail.shape, F32),
            jax.ShapeDtypeStruct(gain.shape, F32),
        ),
        in_specs=[vmem, vmem, vmem, hbm, hbm, vmem, vmem, pl.BlockSpec(memory_space=pltpu.SMEM)],
        out_specs=(vmem, hbm, hbm, vmem, vmem, vmem, vmem, vmem),
        scratch_shapes=[
            pltpu.VMEM((tokens, width), BF16),
            pltpu.VMEM((tokens, width), BF16),
            pltpu.VMEM((channels, width), BF16),
            pltpu.VMEM((channels, width), BF16),
            pltpu.VMEM((tokens + 16, channels), F32),
            pltpu.VMEM((tokens + 8, channels), F32),
            pltpu.VMEM((tokens, channels), BF16),
            pltpu.VMEM((tokens, channels), BF16),
            pltpu.VMEM((tokens, width), BF16),
            pltpu.VMEM((chips, rows, width), BF16),
            pltpu.VMEM((chips + 1, rows, width), BF16),
            pltpu.VMEM((chips, rows, width), BF16),
            pltpu.VMEM((n, 1, width), F32),
            pltpu.VMEM((1, width), F32),
            dma((3, 2, n)),
            dma((2, n)),
            dma((chips,)),
            dma((chips,)),
            dma((cuts, chips)),
            dma((cuts, chips + 1)),
            dma((n,)),
            dma((n,)),
            dma((3,)),
            dma((2,)),
        ],
        compiler_params=pltpu.CompilerParams(
            collective_id=0, has_side_effects=True, vmem_limit_bytes=60 * 2**20
        ),
    )(x_in, grad_out, gain, w_val, w_out, filt, tail, micro_index)
    route = [(i, (i - 1) % sections) for i in range(sections)]
    received = lax.ppermute(grad_local, "section", route)
    return (
        received[None],
        dot_nn(gv_t, normed).astype(BF16)[None],
        dot_nn(gat_t, cot).astype(BF16)[None],
        grad_filter,
        grad_tail,
        grad_gain,
    )


def solution(mesh):
    placed = (
        P("section", "tensor", None),
        P("section", "tensor", None),
        P("section", None),
        P("section", "tensor", None),
        P("section", "tensor", None),
        P("section", None, "tensor"),
        P("section", None, "tensor"),
        P("section"),
    )
    return jax.shard_map(
        functools.partial(on_device, mesh.shape["tensor"], mesh.shape["section"]),
        mesh=mesh,
        in_specs=placed,
        out_specs=(
            P("section", "tensor", None),
            P("section", "tensor", None),
            P("section", "tensor", None),
            P("section", None, "tensor"),
            P("section", None, "tensor"),
            P("section", None),
        ),
        check_vma=False,
    )
```

time: 214 us -> 133 us (0.62)
  the two profiles are of different devices: /device:TPU:0 before, /device:TPU:12 now
where the time goes in v2:
time: 133 us; the launch traced here: 131 us
  Pallas kernels  112 us (84%)
  matrix products  11.2 us (8%)
  local copies, waits for them, and re-layouts  4.59 us (3%)
  starting transfers between devices  1.69 us (1%)
    pallas_call x1, Pallas kernels, on_device(): pl.pallas_call(functools.partial(kernel, n, 512), out_shape=(jax.ShapeDty...  112 us
    dot_general x2, matrix products, dot_nn(): lax.dot_general(left, right, (((1,), (0,)), ((), ())), preferred_element_...  11.2 us
    unnamed x13, local copies, waits for them, and re-layouts  4.59 us
  transfers between devices with their start and end apart: 1, of which 0 were waited for; matrix products, arithmetic and copies ran while one was open for 10% of the time, Pallas kernels for 0%

profile of v2, /device:TPU:12, one launch (start us, length us, event | category | flops | bytes accessed | tf_op | source)
XLA Modules:
  0.0 131.1 jit_solution(13920980608453523941)
XLA Ops:
  1.3 1.3 copy.14.filt_ref
  2.6 112.3 %shard_map.127 = (bf16[64,4096]{1,0:T(8,128)(2,1)}, bf16[512,4096]{1,0:T(8,128)(2,1)}, bf16[512,4096]{1,0:T(8,128)(2,1)}, bf16[512,512]{1,0:T(8,128)(2,1)}, bf16...) custom-call(bf16[1,64,4096]{2,1,0:T(8,128)(2,1)} %x_ref.1, ...), custom_call_target="tpu_custom_call" | custom-call | tf_op jit(solution)/shard_map/pallas_call | solution.py:412
  114.9 1.7 %collective-permute-start = (bf16[64,4096]{1,0:T(8,128)(2,1)}, bf16[64,4096]{1,0:T(8,128)(2,1)S(1)}, u32[]{:S(2)}, u32[]{:S(2)}) collective-permute-start(bf16[64,4096]{1,0:T(8,128)(2,1)} %get-tuple-element.14), channel_id=1, source_target_pairs={{0,24},{8,0},{16,8},{24,16},{1,25},{9,1},{17,9},{25,17},{2,26},{10... | collective-permute-start | bytes 1572872 | tf_op jit(solution)/shard_map/ppermute | solution.py:457
  116.6 1.3 copy.15
  117.9 0.0 copy-start.2
  117.9 0.0 copy-start.3
  117.9 6.9 %fusion = bf16[1,512,4096]{2,1,0:T(8,128)(2,1)} fusion(bf16[512,512]{1,0:T(8,128)(2,1)} %get-tuple-element.15, bf16[512,4096]{1,0:T(8,128)(2,1)} %get-tuple-element.16), kind=kOutput, calls=%fused_computation.2 | convolution fusion | flops 2149580800 | bytes 8912896 | tf_op jit(solution)/shard_map/dot_general | solution.py:22
  124.7 0.0 copy-done.2
  124.7 0.0 copy-done.3
  124.8 0.0 copy-start.1
  124.8 0.0 copy-start
  124.8 4.4 %fusion.1 = bf16[1,512,4096]{2,1,0:T(8,128)(2,1)} fusion(bf16[512,512]{1,0:T(8,128)(2,1)S(1)} %copy-done.3, bf16[512,4096]{1,0:T(8,128)(2,1)S(1)} %copy-done.2), kind=kOutput, calls=%fused_computation.3 | convolution fusion | flops 2149580800 | bytes 8912896 | tf_op jit(solution)/shard_map/dot_general | solution.py:22
  129.1 0.0 collective-permute-done
  129.1 0.8 copy.20
  129.9 0.0 copy-done.1
  129.9 0.6 copy.21
  130.5 0.0 copy-done
  130.5 0.6 copy.22
Async XLA Ops:
  114.9 14.2 %collective-permute-start = (bf16[64,4096]{1,0:T(8,128)(2,1)}, bf16[64,4096]{1,0:T(8,128)(2,1)S(1)}, u32[]{:S(2)}, u32[]{:S(2)}) collective-permute-start(bf16[64,4096]{1,0:T(8,128)(2,1)} %get-tuple-element.14), channel_id=1, source_target_pairs={{0,24},{8,0},{16,8},{24,16},{1,25},{9,1},{17,9},{25,17},{2,26},{10... | collective-permute-start | bytes 1572872 | tf_op jit(solution)/shard_map/ppermute | solution.py:457
  117.9 6.9 %copy-start.2 = (bf16[512,4096]{1,0:T(8,128)(2,1)S(1)}, bf16[512,4096]{1,0:T(8,128)(2,1)}, u32[]{:S(2)}) copy-start(bf16[512,4096]{1,0:T(8,128)(2,1)} %get-tuple-element.18) | copy-start | bytes 12582916
  117.9 6.9 %copy-start.3 = (bf16[512,512]{1,0:T(8,128)(2,1)S(1)}, bf16[512,512]{1,0:T(8,128)(2,1)}, u32[]{:S(2)}) copy-start(bf16[512,512]{1,0:T(8,128)(2,1)} %get-tuple-element.17) | copy-start | bytes 1572868
  124.8 5.2 %copy-start.1 = (f32[1,2,512]{2,1,0:T(2,128)S(1)}, f32[1,2,512]{2,1,0:T(2,128)}, u32[]{:S(2)}) copy-start(f32[1,2,512]{2,1,0:T(2,128)} %get-tuple-element.38) | copy-start | bytes 12292
  124.8 5.8 %copy-start = (f32[1,4096]{1,0:T(1,128)S(1)}, f32[1,4096]{1,0:T(1,128)}, u32[]{:S(2)}) copy-start(f32[1,4096]{1,0:T(1,128)} %get-tuple-element.39) | copy-start | bytes 49156

commit v3 on v2

--- a/solution.py
+++ b/solution.py
@@ -23,12 +23,12 @@
 
 
 def kernel(
-    n, col_tile,
+    n, sections, col_tile,
     x_ref, cot_ref, gain_ref, wv_hbm, wo_hbm, filt_ref, tail_ref, micro_ref,
-    gloc_out, nrm_out, got_out, gat_t, gv_t, gfilt_out, gtail_out, ggain_out,
-    nrm, got, wv, wo, vals, gg, gat, gv, part, sib, inc, outg, gparts, own,
+    gin_out, gwv_out, gwo_out, gfilt_out, gtail_out, ggain_out,
+    nrm, got, wv, wo, vals, gg, gat, gv, gat_t, gv_t, gwo, gwv, gloc, part, sib, inc, outg, gparts, own,
     ag_send, ag_recv, sib_send, sib_recv, line_send, line_recv,
-    gain_send, gain_recv, load_sem, store_sem,
+    gain_send, gain_recv, load_sem, store_sem, shift_send, shift_recv,
 ):
     chips = n // 2
     rows = x_ref.shape[1]
@@ -43,6 +43,9 @@
     z = me // 2
     c = me % 2
     other = z * 2 + (1 - c)
+    sec = lax.axis_index("section")
+    sec_prev = lax.rem(sec + sections - 1, sections)
+    sec_next = lax.rem(sec + 1, sections)
 
     def rows_of(d):
         return pl.ds(pl.multiple_of(d * rows, rows), rows)
@@ -66,6 +69,8 @@
         return 0
 
     lax.fori_loop(1, n, greet, 0)
+    pl.semaphore_signal(barrier, inc=1, device_id={"section": sec_prev}, device_id_type=MESH)
+    pl.semaphore_signal(barrier, inc=1, device_id={"section": sec_next}, device_id_type=MESH)
 
     x_float = x_ref[0].astype(F32)
     inv_rms = lax.rsqrt(jnp.mean(x_float * x_float, axis=-1, keepdims=True) + EPSILON)
@@ -77,7 +82,7 @@
     vals[tokens + 8 : tokens + 16, :] = jnp.zeros((8, channels), F32)
     gg[tokens : tokens + 8, :] = jnp.zeros((8, channels), F32)
     gfilt_out[...] = jnp.zeros_like(gfilt_out)
-    pl.semaphore_wait(barrier, n - 1)
+    pl.semaphore_wait(barrier, n + 1)
 
     gathered = (got, nrm)
 
@@ -150,7 +155,7 @@
         def strip(i, _):
             cs = pl.ds(pl.multiple_of(i * 128, 128), 128)
             window = vals[pl.ds(first, rows + 16), cs]
-            f = [filt_ref[0, k : k + 1, cs] for k in range(TAPS)]
+            f = [filt_ref[k, :, cs] for k in range(TAPS)]
             v = window[8:]
             v1 = pltpu.roll(window, 1, 0)[8:]
             v2 = pltpu.roll(window, 2, 0)[8:]
@@ -162,7 +167,7 @@
             gc2 = pltpu.roll(gc, rows + 6, 0)[:rows]
             here = gc[:rows]
             for k, shifted in enumerate((v, v1, v2)):
-                gfilt_out[0, k : k + 1, cs] += jnp.sum(here * shifted[:rows], axis=0, keepdims=True)
+                gfilt_out[k, :, cs] += jnp.sum(here * shifted[:rows], axis=0, keepdims=True)
             gv[rows_of(d), cs] = (f[0] * here + f[1] * gc1 + f[2] * gc2).astype(BF16)
 
             @pl.when(d == 0)
@@ -268,13 +273,10 @@
             device_id_type=MESH,
         )
 
-    store_nrm = pltpu.make_async_copy(nrm, nrm_out, store_sem.at[0])
-    store_got = pltpu.make_async_copy(got, got_out, store_sem.at[1])
+    store_wo = pltpu.make_async_copy(gwo, gwo_out, store_sem.at[0])
+    store_wv = pltpu.make_async_copy(gwv, gwv_out, store_sem.at[1])
 
     def gain_part():
-        store_nrm.start()
-        store_got.start()
-
         def turned(i, _):
             cs = pl.ds(pl.multiple_of(i * 128, 128), 128)
             gat_t[cs, :] = gat[:, cs].astype(F32).T.astype(BF16)
@@ -286,12 +288,14 @@
         def tile(j, _):
             cols = pl.ds(pl.multiple_of(j * col_tile, col_tile), col_tile)
             grad = dot_nn(gv_t[...], nrm[:, cols])
+            gwv[:, cols] = grad.astype(BF16)
             own[:, cols] = (
                 jnp.sum(grad * wv[:, cols].astype(F32), axis=0, keepdims=True) / gain_ref[:, cols]
             )
             return 0
 
         lax.fori_loop(0, width // col_tile, tile, 0)
+        store_wv.start()
         gparts[me] = own[...]
 
         def send(k, _):
@@ -299,6 +303,14 @@
             return 0
 
         lax.fori_loop(1, n, send, 0)
+
+        def out_tile(j, _):
+            cols = pl.ds(pl.multiple_of(j * col_tile, col_tile), col_tile)
+            gwo[:, cols] = dot_nn(gat_t[...], got[:, cols]).astype(BF16)
+            return 0
+
+        lax.fori_loop(0, width // col_tile, out_tile, 0)
+        store_wo.start()
 
     def process(s, low, high):
         project_at(1, s)
@@ -345,6 +357,16 @@
     @pl.when(jnp.logical_not(inner))
     def _():
         gain_part()
+
+    def shift_copy(q):
+        return pltpu.make_async_remote_copy(
+            src_ref=gloc.at[piece_of(q)],
+            dst_ref=gin_out.at[piece_of(q)],
+            send_sem=shift_send.at[q],
+            recv_sem=shift_recv.at[q],
+            device_id={"section": sec_prev},
+            device_id_type=MESH,
+        )
 
     sib_copy(z).wait_recv()
 
@@ -363,9 +385,10 @@
         x_now = x_ref[0, piece_of(q), :].astype(F32)
         inv = lax.rsqrt(jnp.mean(x_now * x_now, axis=-1, keepdims=True) + EPSILON)
         dots = jnp.mean(scaled * x_now, axis=-1, keepdims=True)
-        gloc_out[piece_of(q), :] = (
+        gloc[piece_of(q), :] = (
             cot_ref[0, piece_of(q), :].astype(F32) + inv * scaled - x_now * (inv**3 * dots)
         ).astype(BF16)
+        shift_copy(q).start()
         return 0
 
     lax.fori_loop(0, cuts, finish, 0)
@@ -396,8 +419,31 @@
         return 0
 
     lax.fori_loop(0, cuts * chips, line_drain, 0)
-    store_nrm.wait()
-    store_got.wait()
+    store_wo.wait()
+    store_wv.wait()
+
+    def shift_wait(q, _):
+        shift_copy(q).wait()
+        return 0
+
+    lax.fori_loop(0, cuts, shift_wait, 0)
+
+
+def hand_on(splits, *refs):
+    count = len(splits)
+    sems = refs[2 * count]
+    copies = []
+    for source, target, parts in zip(refs[:count], refs[count : 2 * count], splits):
+        height = source.shape[0] // parts
+        for i in range(parts):
+            cut = pl.ds(i * height, height)
+            copies.append(
+                pltpu.make_async_copy(source.at[cut], target.at[cut], sems.at[len(copies)])
+            )
+    for copy in copies:
+        copy.start()
+    for copy in copies:
+        copy.wait()
 
 
 def on_device(n, sections, x_in, grad_out, gain, w_val, w_out, filt, tail, micro_index):
@@ -409,20 +455,19 @@
     vmem = pl.BlockSpec(memory_space=pltpu.VMEM)
     hbm = pl.BlockSpec(memory_space=pl.ANY)
     dma = pltpu.SemaphoreType.DMA
-    grad_local, normed, cot, gat_t, gv_t, grad_filter, grad_tail, grad_gain = pl.pallas_call(
-        functools.partial(kernel, n, 512),
-        out_shape=(
-            jax.ShapeDtypeStruct((rows, width), BF16),
-            jax.ShapeDtypeStruct((tokens, width), BF16),
-            jax.ShapeDtypeStruct((tokens, width), BF16),
-            jax.ShapeDtypeStruct((channels, tokens), BF16),
-            jax.ShapeDtypeStruct((channels, tokens), BF16),
-            jax.ShapeDtypeStruct(filt.shape, F32),
-            jax.ShapeDtypeStruct(tail.shape, F32),
-            jax.ShapeDtypeStruct(gain.shape, F32),
-        ),
+    shapes = (
+        jax.ShapeDtypeStruct((rows, width), BF16),
+        jax.ShapeDtypeStruct((channels, width), BF16),
+        jax.ShapeDtypeStruct((channels, width), BF16),
+        jax.ShapeDtypeStruct((TAPS, 1, channels), F32),
+        jax.ShapeDtypeStruct(tail.shape, F32),
+        jax.ShapeDtypeStruct(gain.shape, F32),
+    )
+    results = pl.pallas_call(
+        functools.partial(kernel, n, sections, 512),
+        out_shape=shapes,
         in_specs=[vmem, vmem, vmem, hbm, hbm, vmem, vmem, pl.BlockSpec(memory_space=pltpu.SMEM)],
-        out_specs=(vmem, hbm, hbm, vmem, vmem, vmem, vmem, vmem),
+        out_specs=(hbm, hbm, hbm, vmem, vmem, vmem),
         scratch_shapes=[
             pltpu.VMEM((tokens, width), BF16),
             pltpu.VMEM((tokens, width), BF16),
@@ -432,6 +477,11 @@
             pltpu.VMEM((tokens + 8, channels), F32),
             pltpu.VMEM((tokens, channels), BF16),
             pltpu.VMEM((tokens, channels), BF16),
+            pltpu.VMEM((channels, tokens), BF16),
+            pltpu.VMEM((channels, tokens), BF16),
+            pltpu.VMEM((channels, width), BF16),
+            pltpu.VMEM((channels, width), BF16),
+            pltpu.VMEM((rows, width), BF16),
             pltpu.VMEM((tokens, width), BF16),
             pltpu.VMEM((chips, rows, width), BF16),
             pltpu.VMEM((chips + 1, rows, width), BF16),
@@ -448,18 +498,27 @@
             dma((n,)),
             dma((3,)),
             dma((2,)),
+            dma((cuts,)),
+            dma((cuts,)),
         ],
         compiler_params=pltpu.CompilerParams(
             collective_id=0, has_side_effects=True, vmem_limit_bytes=60 * 2**20
         ),
-    )(x_in, grad_out, gain, w_val, w_out, filt, tail, micro_index)
-    route = [(i, (i - 1) % sections) for i in range(sections)]
-    received = lax.ppermute(grad_local, "section", route)
+    )(x_in, grad_out, gain, w_val, w_out, filt.transpose(1, 0, 2), tail, micro_index)
+    splits = (1, 4, 4, 1, 1, 1)
+    grad_in, grad_wv, grad_wo, grad_filter, grad_tail, grad_gain = pl.pallas_call(
+        functools.partial(hand_on, splits),
+        out_shape=shapes,
+        in_specs=[hbm] * len(shapes),
+        out_specs=(hbm,) * len(shapes),
+        scratch_shapes=[dma((sum(splits),))],
+        compiler_params=pltpu.CompilerParams(vmem_limit_bytes=60 * 2**20),
+    )(*results)
     return (
-        received[None],
-        dot_nn(gv_t, normed).astype(BF16)[None],
-        dot_nn(gat_t, cot).astype(BF16)[None],
-        grad_filter,
+        grad_in[None],
+        grad_wv[None],
+        grad_wo[None],
+        grad_filter.transpose(1, 0, 2),
         grad_tail,
         grad_gain,
     )

time: 133 us -> 393 us (2.95)
  Pallas kernels: 112 us -> 392 us
  matrix products: 11.2 us -> 0 us
  local copies, waits for them, and re-layouts: 4.59 us -> 0 us
    pallas_call x1 -> x2, Pallas kernels: 112 us -> 392 us  [the longest x1 272 us: on_device(): pl.pallas_call(functools.partial(hand_on, splits), out_shape=shapes, in_s...]
    dot_general x2 -> x0, matrix products: 11.2 us -> none  [dot_nn(): lax.dot_general(left, right, (((1,), (0,)), ((), ())), preferred_element_...]
    unnamed x13 -> x0, local copies, waits for them, and re-layouts: 4.59 us -> none
  transfers between devices with their start and end apart: 1 -> 0, of which waited for: 0 -> 0; matrix products, arithmetic and copies ran while one was open for 10% -> 0% of each run, Pallas kernels for 0% -> 0%
where the time goes in v3:
time: 393 us
  Pallas kernels  392 us (100%)
    pallas_call x1, Pallas kernels, on_device(): pl.pallas_call(functools.partial(hand_on, splits), out_shape=shapes, in_s...  272 us
    pallas_call x1, Pallas kernels, on_device(): pl.pallas_call(functools.partial(kernel, n, sections, 512), out_shape=sha...  120 us

profile of v3, /device:TPU:12, one launch (start us, length us, event | category | flops | bytes accessed | tf_op | source)
XLA Modules:
  0.0 393.1 jit_solution(5887077903403500401)
XLA Ops:
  1.3 119.8 %shard_map.127 = (bf16[64,4096]{1,0:T(8,128)(2,1)}, bf16[512,4096]{1,0:T(8,128)(2,1)}, bf16[512,4096]{1,0:T(8,128)(2,1)}, f32[3,1,512]{2,1,0:T(1,128)}, f32[1,2,512]{2,1,0:T(2,128)}, /*index=5*/f32[1,4096]{1,0:T(1,128)}) custom-call(bf16[1,64,4096]{2,1,0:T(8,128)(2,1)} %x_ref.1, bf16[1,64,4096]{2,1,0:T(8,128)(2,1)} %cot_ref.1, f32[1,4096]{1,0:T(1,128)} %gain_ref.1, ...), custom_call_target="tpu_custom_call" | custom-call | tf_op jit(solution)/shard_map/pallas_call | solution.py:466
  121.1 272.0 %shard_map.128 = (bf16[64,4096]{1,0:T(8,128)(2,1)}, bf16[512,4096]{1,0:T(8,128)(2,1)}, bf16[512,4096]{1,0:T(8,128)(2,1)}, f32[3,1,512]{2,1,0:T(1,128)}, f32[1,2,512]{2,1,0:T(2,128)}, /*index=5*/f32[1,4096]{1,0:T(1,128)}) custom-call(bf16[64,4096]{1,0:T(8,128)(2,1)} %get-tuple-element.18.refs_0_, bf16[512,4096]{1,0:T(8,128)(2,1)} %get-tuple-element.19.refs_1_, ...), custom_call_target="tpu_custom_call" | custom-call | tf_op jit(solution)/shard_map/pallas_call | solution.py:509

commit v4 on v3

--- a/solution.py
+++ b/solution.py
@@ -431,19 +431,23 @@
 
 def hand_on(splits, *refs):
     count = len(splits)
-    sems = refs[2 * count]
-    copies = []
-    for source, target, parts in zip(refs[:count], refs[count : 2 * count], splits):
+    staged = refs[2 * count : 3 * count]
+    sem_in, sem_out = refs[3 * count :]
+    reads, writes = [], []
+    for source, stage, target, parts in zip(refs[:count], staged, refs[count : 2 * count], splits):
         height = source.shape[0] // parts
         for i in range(parts):
             cut = pl.ds(i * height, height)
-            copies.append(
-                pltpu.make_async_copy(source.at[cut], target.at[cut], sems.at[len(copies)])
-            )
-    for copy in copies:
-        copy.start()
-    for copy in copies:
-        copy.wait()
+            at = len(reads)
+            reads.append(pltpu.make_async_copy(source.at[cut], stage.at[cut], sem_in.at[at]))
+            writes.append(pltpu.make_async_copy(stage.at[cut], target.at[cut], sem_out.at[at]))
+    for read in reads:
+        read.start()
+    for read, write in zip(reads, writes):
+        read.wait()
+        write.start()
+    for write in writes:
+        write.wait()
 
 
 def on_device(n, sections, x_in, grad_out, gain, w_val, w_out, filt, tail, micro_index):
@@ -505,13 +509,14 @@
             collective_id=0, has_side_effects=True, vmem_limit_bytes=60 * 2**20
         ),
     )(x_in, grad_out, gain, w_val, w_out, filt.transpose(1, 0, 2), tail, micro_index)
-    splits = (1, 4, 4, 1, 1, 1)
+    splits = (1, 8, 8, 1, 1, 1)
     grad_in, grad_wv, grad_wo, grad_filter, grad_tail, grad_gain = pl.pallas_call(
         functools.partial(hand_on, splits),
         out_shape=shapes,
         in_specs=[hbm] * len(shapes),
         out_specs=(hbm,) * len(shapes),
-        scratch_shapes=[dma((sum(splits),))],
+        scratch_shapes=[pltpu.VMEM(shape.shape, shape.dtype) for shape in shapes]
+        + [dma((sum(splits),)), dma((sum(splits),))],
         compiler_params=pltpu.CompilerParams(vmem_limit_bytes=60 * 2**20),
     )(*results)
     return (

time: 393 us -> 128 us (0.33)
  Pallas kernels: 392 us -> 127 us
    pallas_call x1, Pallas kernels: 272 us -> 7.13 us  [on_device(): pl.pallas_call(functools.partial(hand_on, splits), out_shape=shapes, in_s...]
where the time goes in v4:
time: 128 us
  Pallas kernels  127 us (99%)
  between operations  1.29 us (1%)
    pallas_call x1, Pallas kernels, on_device(): pl.pallas_call(functools.partial(kernel, n, sections, 512), out_shape=sha...  120 us
    pallas_call x1, Pallas kernels, on_device(): pl.pallas_call(functools.partial(hand_on, splits), out_shape=shapes, in_s...  7.13 us

profile of v4, /device:TPU:12, one launch (start us, length us, event | category | flops | bytes accessed | tf_op | source)
XLA Modules:
  0.0 128.3 jit_solution(8384809852346640811)
XLA Ops:
  1.3 119.8 %shard_map.127 = (bf16[64,4096]{1,0:T(8,128)(2,1)}, bf16[512,4096]{1,0:T(8,128)(2,1)}, bf16[512,4096]{1,0:T(8,128)(2,1)}, f32[3,1,512]{2,1,0:T(1,128)}, f32[1,2,512]{2,1,0:T(2,128)}, /*index=5*/f32[1,4096]{1,0:T(1,128)}) custom-call(bf16[1,64,4096]{2,1,0:T(8,128)(2,1)} %x_ref.1, bf16[1,64,4096]{2,1,0:T(8,128)(2,1)} %cot_ref.1, f32[1,4096]{1,0:T(1,128)} %gain_ref.1, ...), custom_call_target="tpu_custom_call" | custom-call | tf_op jit(solution)/shard_map/pallas_call | solution.py:470
  121.1 7.1 %shard_map.128 = (bf16[64,4096]{1,0:T(8,128)(2,1)}, bf16[512,4096]{1,0:T(8,128)(2,1)}, bf16[512,4096]{1,0:T(8,128)(2,1)}, f32[3,1,512]{2,1,0:T(1,128)}, f32[1,2,512]{2,1,0:T(2,128)}, /*index=5*/f32[1,4096]{1,0:T(1,128)}) custom-call(bf16[64,4096]{1,0:T(8,128)(2,1)} %get-tuple-element.18.refs_0_, bf16[512,4096]{1,0:T(8,128)(2,1)} %get-tuple-element.19.refs_1_, ...), custom_call_target="tpu_custom_call" | custom-call | tf_op jit(solution)/shard_map/pallas_call | solution.py:513

commit v5 on v3

--- a/solution.py
+++ b/solution.py
@@ -25,10 +25,10 @@
 def kernel(
     n, sections, col_tile,
     x_ref, cot_ref, gain_ref, wv_hbm, wo_hbm, filt_ref, tail_ref, micro_ref,
-    gin_out, gwv_out, gwo_out, gfilt_out, gtail_out, ggain_out,
-    nrm, got, wv, wo, vals, gg, gat, gv, gat_t, gv_t, gwo, gwv, gloc, part, sib, inc, outg, gparts, own,
+    gin_out, gwv, gwo, gfilt_out, gtail_out, ggain_out,
+    nrm, got, wv, wo, vals, gg, gat, gv, gat_t, gv_t, gloc, part, sib, inc, outg, gparts, own,
     ag_send, ag_recv, sib_send, sib_recv, line_send, line_recv,
-    gain_send, gain_recv, load_sem, store_sem, shift_send, shift_recv,
+    gain_send, gain_recv, load_sem, shift_send, shift_recv,
 ):
     chips = n // 2
     rows = x_ref.shape[1]
@@ -259,9 +259,23 @@
 
         lax.fori_loop(0, cuts, turn, 0)
 
-    def shares(s, low, high):
-        lax.fori_loop(low_end(s), low, share, 0)
-        lax.fori_loop(high, high_end(s), share, 0)
+    def shares_and_sums(s, low, high):
+        below = low - low_end(s)
+        above = high_end(s) - high
+        late_below = jnp.where((s == last) & (below > 0), 1, 0)
+        late_above = jnp.where((s == last) & (above > 0), 1, 0)
+        first = below - late_below
+
+        def outer_share(k, _):
+            return share(jnp.where(k < first, low_end(s) + k, high_end(s) - 1 - (k - first)), 0)
+
+        lax.fori_loop(0, first + above - late_above, outer_share, 0)
+        windows(s)
+
+        def inner_share(k, _):
+            return share(jnp.where(k < late_below, low - 1, high), 0)
+
+        lax.fori_loop(0, late_below + late_above, inner_share, 0)
 
     def gain_copy(k, d):
         return pltpu.make_async_remote_copy(
@@ -273,8 +287,6 @@
             device_id_type=MESH,
         )
 
-    store_wo = pltpu.make_async_copy(gwo, gwo_out, store_sem.at[0])
-    store_wv = pltpu.make_async_copy(gwv, gwv_out, store_sem.at[1])
 
     def gain_part():
         def turned(i, _):
@@ -295,7 +307,6 @@
             return 0
 
         lax.fori_loop(0, width // col_tile, tile, 0)
-        store_wv.start()
         gparts[me] = own[...]
 
         def send(k, _):
@@ -310,12 +321,10 @@
             return 0
 
         lax.fori_loop(0, width // col_tile, out_tile, 0)
-        store_wo.start()
 
     def process(s, low, high):
         project_at(1, s)
-        shares(s, low, high)
-        windows(s)
+        shares_and_sums(s, low, high)
 
     inner = (z > 0) & (z < last)
     project_at(0, 0)
@@ -419,8 +428,6 @@
         return 0
 
     lax.fori_loop(0, cuts * chips, line_drain, 0)
-    store_wo.wait()
-    store_wv.wait()
 
     def shift_wait(q, _):
         shift_copy(q).wait()
@@ -465,9 +472,9 @@
     )
     results = pl.pallas_call(
         functools.partial(kernel, n, sections, 512),
-        out_shape=shapes,
+        out_shape=shapes[:1] + tuple(pltpu.VMEM(shape.shape, shape.dtype) for shape in shapes[1:]),
         in_specs=[vmem, vmem, vmem, hbm, hbm, vmem, vmem, pl.BlockSpec(memory_space=pltpu.SMEM)],
-        out_specs=(hbm, hbm, hbm, vmem, vmem, vmem),
+        out_specs=(hbm, vmem, vmem, vmem, vmem, vmem),
         scratch_shapes=[
             pltpu.VMEM((tokens, width), BF16),
             pltpu.VMEM((tokens, width), BF16),
@@ -479,8 +486,6 @@
             pltpu.VMEM((tokens, channels), BF16),
             pltpu.VMEM((channels, tokens), BF16),
             pltpu.VMEM((channels, tokens), BF16),
-            pltpu.VMEM((channels, width), BF16),
-            pltpu.VMEM((channels, width), BF16),
             pltpu.VMEM((rows, width), BF16),
             pltpu.VMEM((tokens, width), BF16),
             pltpu.VMEM((chips, rows, width), BF16),
@@ -497,22 +502,21 @@
             dma((n,)),
             dma((n,)),
             dma((3,)),
-            dma((2,)),
             dma((cuts,)),
             dma((cuts,)),
         ],
         compiler_params=pltpu.CompilerParams(
-            collective_id=0, has_side_effects=True, vmem_limit_bytes=60 * 2**20
+            collective_id=0, has_side_effects=True, vmem_limit_bytes=50 * 2**20
         ),
     )(x_in, grad_out, gain, w_val, w_out, filt.transpose(1, 0, 2), tail, micro_index)
-    splits = (1, 4, 4, 1, 1, 1)
+    splits = (1, 8, 8, 1, 1, 1)
     grad_in, grad_wv, grad_wo, grad_filter, grad_tail, grad_gain = pl.pallas_call(
         functools.partial(hand_on, splits),
         out_shape=shapes,
-        in_specs=[hbm] * len(shapes),
+        in_specs=[vmem] * len(shapes),
         out_specs=(hbm,) * len(shapes),
         scratch_shapes=[dma((sum(splits),))],
-        compiler_params=pltpu.CompilerParams(vmem_limit_bytes=60 * 2**20),
+        compiler_params=pltpu.CompilerParams(vmem_limit_bytes=16 * 2**20),
     )(*results)
     return (
         grad_in[None],

time: 393 us -> 123 us (0.31)
  Pallas kernels: 392 us -> 121 us
    pallas_call x1, Pallas kernels: 272 us -> 3.61 us  [on_device(): pl.pallas_call(functools.partial(hand_on, splits), out_shape=shapes, in_s...]
where the time goes in v5:
time: 123 us
  Pallas kernels  121 us (98%)
  between operations  1.3 us (1%)
    pallas_call x1, Pallas kernels, on_device(): pl.pallas_call(functools.partial(kernel, n, sections, 512), out_shape=sha...  117 us
    pallas_call x1, Pallas kernels, on_device(): pl.pallas_call(functools.partial(hand_on, splits), out_shape=shapes, in_s...  3.61 us

profile of v5, /device:TPU:12, one launch (start us, length us, event | category | flops | bytes accessed | tf_op | source)
XLA Modules:
  0.0 123.1 jit_solution(15506014560836085283)
XLA Ops:
  1.3 117.2 %shard_map.127 = (bf16[64,4096]{1,0:T(8,128)(2,1)}, bf16[512,4096]{1,0:T(8,128)(2,1)S(1)}, bf16[512,4096]{1,0:T(8,128)(2,1)S(1)}, f32[3,1,512]{2,1,0:T(1,128)S(1...) custom-call(bf16[1,64,4096]{2,1,0:T(8,128)(2,1)} %x_ref.1, bf16[1,64,4096]{2,1,0:T(8,128)(2,1)} %cot_ref.1, ...), custom_call_target="tpu_custom_call" | custom-call | tf_op jit(solution)/shard_map/pallas_call | solution.py:473
  118.4 0.0 copy-start
  118.5 1.0 copy-done
  119.5 3.6 %shard_map.128 = (bf16[64,4096]{1,0:T(8,128)(2,1)}, bf16[512,4096]{1,0:T(8,128)(2,1)}, bf16[512,4096]{1,0:T(8,128)(2,1)}, f32[3,1,512]{2,1,0:T(1,128)}, f32[1,2,512]{2,1,0:T(2,128)}, /*index=5*/f32[1,4096]{1,0:T(1,128)}) custom-call(bf16[64,4096]{1,0:T(8,128)(2,1)S(1)} %copy-done, bf16[512,4096]{1,0:T(8,128)(2,1)S(1)} %get-tuple-element.19.refs_1_, ...), custom_call_target="tpu_custom_call" | custom-call | tf_op jit(solution)/shard_map/pallas_call | solution.py:513
Async XLA Ops:
  118.4 1.0 copy-start

commit v6 on v5

--- a/solution.py
+++ b/solution.py
@@ -149,26 +149,28 @@
             device_id_type=MESH,
         )
 
-    def share(d, _):
+    def share(d, blocks):
+        height = blocks * rows
         first = pl.multiple_of(d * rows, rows)
+        span = pl.ds(first, height)
 
         def strip(i, _):
             cs = pl.ds(pl.multiple_of(i * 128, 128), 128)
-            window = vals[pl.ds(first, rows + 16), cs]
+            window = vals[pl.ds(first, height + 16), cs]
             f = [filt_ref[k, :, cs] for k in range(TAPS)]
             v = window[8:]
             v1 = pltpu.roll(window, 1, 0)[8:]
             v2 = pltpu.roll(window, 2, 0)[8:]
             conv = f[0] * v + f[1] * v1 + f[2] * v2
             sig = jax.nn.sigmoid(conv)
-            gat[rows_of(d), cs] = (conv * sig)[:rows].astype(BF16)
-            gc = gg[pl.ds(first, rows + 8), cs] * sig * (1.0 + conv * (1.0 - sig))
-            gc1 = pltpu.roll(gc, rows + 7, 0)[:rows]
-            gc2 = pltpu.roll(gc, rows + 6, 0)[:rows]
-            here = gc[:rows]
+            gat[span, cs] = (conv * sig)[:height].astype(BF16)
+            gc = gg[pl.ds(first, height + 8), cs] * sig * (1.0 + conv * (1.0 - sig))
+            gc1 = pltpu.roll(gc, height + 7, 0)[:height]
+            gc2 = pltpu.roll(gc, height + 6, 0)[:height]
+            here = gc[:height]
             for k, shifted in enumerate((v, v1, v2)):
-                gfilt_out[k, :, cs] += jnp.sum(here * shifted[:rows], axis=0, keepdims=True)
-            gv[rows_of(d), cs] = (f[0] * here + f[1] * gc1 + f[2] * gc2).astype(BF16)
+                gfilt_out[k, :, cs] += jnp.sum(here * shifted[:height], axis=0, keepdims=True)
+            gv[span, cs] = (f[0] * here + f[1] * gc1 + f[2] * gc2).astype(BF16)
 
             @pl.when(d == 0)
             def _():
@@ -181,16 +183,16 @@
 
         def tile(j, _):
             cols = pl.ds(pl.multiple_of(j * col_tile, col_tile), col_tile)
-            part[rows_of(d), cols] = dot_nn(gv[rows_of(d), :], wv[:, cols]).astype(BF16)
+            part[span, cols] = dot_nn(gv[span, :], wv[:, cols]).astype(BF16)
             return 0
 
         lax.fori_loop(0, width // col_tile, tile, 0)
 
-        @pl.when(d % 2 != c)
-        def _():
-            sib_copy(d // 2).start()
-
-        return 0
+        given = jnp.where(d % 2 != c, d, d + 1)
+
+        @pl.when(given < d + blocks)
+        def _():
+            sib_copy(given // 2).start()
 
     def low_end(s):
         lo = z - s
@@ -262,20 +264,26 @@
     def shares_and_sums(s, low, high):
         below = low - low_end(s)
         above = high_end(s) - high
-        late_below = jnp.where((s == last) & (below > 0), 1, 0)
-        late_above = jnp.where((s == last) & (above > 0), 1, 0)
-        first = below - late_below
-
-        def outer_share(k, _):
-            return share(jnp.where(k < first, low_end(s) + k, high_end(s) - 1 - (k - first)), 0)
-
-        lax.fori_loop(0, first + above - late_above, outer_share, 0)
+        low_pairs, high_pairs = below // 2, above // 2
+        odd_low, odd_high = below % 2, above % 2
+
+        def pair_share(k, _):
+            share(
+                jnp.where(
+                    k < low_pairs, low_end(s) + 2 * k, high_end(s) - 2 - 2 * (k - low_pairs)
+                ),
+                2,
+            )
+            return 0
+
+        def odd_share(k, _):
+            share(jnp.where(k < odd_low, low - 1, high), 1)
+            return 0
+
+        lax.fori_loop(0, low_pairs + high_pairs, pair_share, 0)
+        lax.fori_loop(0, jnp.where(s < last, odd_low + odd_high, 0), odd_share, 0)
         windows(s)
-
-        def inner_share(k, _):
-            return share(jnp.where(k < late_below, low - 1, high), 0)
-
-        lax.fori_loop(0, late_below + late_above, inner_share, 0)
+        lax.fori_loop(0, jnp.where(s == last, odd_low + odd_high, 0), odd_share, 0)
 
     def gain_copy(k, d):
         return pltpu.make_async_remote_copy(
@@ -472,9 +480,9 @@
     )
     results = pl.pallas_call(
         functools.partial(kernel, n, sections, 512),
-        out_shape=shapes[:1] + tuple(pltpu.VMEM(shape.shape, shape.dtype) for shape in shapes[1:]),
+        out_shape=tuple(pltpu.VMEM(shape.shape, shape.dtype) for shape in shapes),
         in_specs=[vmem, vmem, vmem, hbm, hbm, vmem, vmem, pl.BlockSpec(memory_space=pltpu.SMEM)],
-        out_specs=(hbm, vmem, vmem, vmem, vmem, vmem),
+        out_specs=(vmem,) * len(shapes),
         scratch_shapes=[
             pltpu.VMEM((tokens, width), BF16),
             pltpu.VMEM((tokens, width), BF16),

time: 123 us -> 121 us (0.984)
  no operation moved by 1% of the time
where the time goes in v6:
time: 121 us
  Pallas kernels  120 us (99%)
  between operations  1.29 us (1%)
    pallas_call x1, Pallas kernels, on_device(): pl.pallas_call(functools.partial(kernel, n, sections, 512), out_shape=tup...  116 us
    pallas_call x1, Pallas kernels, on_device(): pl.pallas_call(functools.partial(hand_on, splits), out_shape=shapes, in_s...  3.62 us

profile of v6, /device:TPU:12, one launch (start us, length us, event | category | flops | bytes accessed | tf_op | source)
XLA Modules:
  0.0 121.0 jit_solution(4918326911910393224)
XLA Ops:
  1.3 116.1 %shard_map.127 = (bf16[64,4096]{1,0:T(8,128)(2,1)S(1)}, bf16[512,4096]{1,0:T(8,128)(2,1)S(1)}, bf16[512,4096]{1,0:T(8,128)(2,1)S(1)}, f32[3,1,512]{2,1,0:T(1,128...) custom-call(bf16[1,64,4096]{2,1,0:T(8,128)(2,1)} %x_ref.1, bf16[1,64,4096]{2,1,0:T(8,128)(2,1)} %cot_ref.1, ...), custom_call_target="tpu_custom_call" | custom-call | tf_op jit(solution)/shard_map/pallas_call | solution.py:481
  117.4 3.6 %shard_map.128 = (bf16[64,4096]{1,0:T(8,128)(2,1)}, bf16[512,4096]{1,0:T(8,128)(2,1)}, bf16[512,4096]{1,0:T(8,128)(2,1)}, f32[3,1,512]{2,1,0:T(1,128)}, f32[1,2,512]{2,1,0:T(2,128)}, /*index=5*/f32[1,4096]{1,0:T(1,128)}) custom-call(bf16[64,4096]{1,0:T(8,128)(2,1)S(1)} %get-tuple-element.18.refs_0_, bf16[512,4096]{1,0:T(8,128)(2,1)S(1)} %get-tuple-element.19.refs_1_, ...), custom_call_target="tpu_custom_call" | custom-call | tf_op jit(solution)/shard_map/pallas_call | solution.py:521
